TPU v7x, 32 devices: a whole 2x2x4 slice. The times are simulated.
32 devices in a mesh: pipe: 4 (over y, core), seq: 4 (over z), tp: 2 (over x).
Axes of the slice: x: 2, y: 2, z: 4, core: 2. Of those that a mesh axis runs over, the one named last changes fastest.
Arguments:
- emitted: bfloat16 [4, 512, 8192], P('pipe', 'seq', 'tp'), may hold values from -6 to 6
- cotangent: bfloat16 [4, 512, 8192], P('pipe', 'seq', 'tp'), may hold values from -6 to 6
- b_proj: bfloat16 [4, 512, 512], P('pipe', 'seq', 'tp'), may hold values from -0.26367188 to 0.26367188
- c_proj: bfloat16 [4, 512, 512], P('pipe', 'seq', 'tp'), may hold values from -0.52734375 to 0.52734375
- log_decay: bfloat16 [4, 512, 128], P('pipe', 'seq', 'tp'), may hold values from -1 to 0
- starts: int32 [4, 512], P('pipe', 'seq'), may hold values 0 or 1
- skip: float32 [4, 128], P('pipe', 'tp'), may hold values from 0.5 to 2
Outputs:
- mixed: bfloat16 [4, 512, 8192], P('pipe', 'seq', 'tp')
- input_grad: bfloat16 [4, 512, 8192], P('pipe', 'seq', 'tp')
All inputs are finite; a program needn't handle non-finite values. No bound on the sum of `starts` on one device may be relied on, other than what follows from the above.
Results may differ from a plain program's by a relative error of at most 0.001.
Values may be sent and summed in bfloat16 or wider, within the bound.
A program may use at most 64 MiB of HBM per device.

v0:
```python
import jax
import jax.numpy as jnp
from jax import lax
from jax.sharding import PartitionSpec as P

BLEND_CHANNELS = 128
P_SIZE = 64
N = 128
GROUPS = 4
SPAN = 128


HIGH = lax.Precision.HIGHEST


def from_behind(value, axis, steps):
    count = lax.axis_size(axis)
    leading, last = (max(0, -steps), min(count, count - steps))
    return lax.ppermute(value, axis, [(source, source + steps) for source in range(leading, last)])


def single_terms(inputs, upstream, b_rows, c_rows, decay_rows, opened):
    running = jnp.cumsum(decay_rows, axis=1)
    running_end = running[:, -1]
    opened_sum = jnp.cumsum(opened, axis=1)
    opened_end = opened_sum[:, -1]
    width = inputs.shape[1]
    causal = jnp.arange(width)[:, None] >= jnp.arange(width)[None, :]
    linked = (opened_sum[:, :, None] == opened_sum[:, None, :]) & causal[None]
    spread = running[:, :, None] - running[:, None, :]
    damping = jnp.where(linked[:, :, :, None, None], jnp.exp(jnp.minimum(spread, 0.0)), 0.0)
    intersection = jnp.einsum("ktgn,ksgn->ktsg", c_rows, b_rows, precision=HIGH)
    mixing = damping * intersection[..., None]
    mixed_part = jnp.einsum("ktsge,ksgep->ktgep", mixing, inputs, precision=HIGH)
    grad_part = jnp.einsum("ktsge,ktgep->ksgep", mixing, upstream, precision=HIGH)
    inflow = jnp.exp(running) * (opened_sum == 0.0)[:, :, None, None]
    outflow = (
        jnp.exp(running_end[:, None] - running)
        * (opened_sum == opened_end[:, None])[:, :, None, None]
    )
    through = jnp.exp(running_end) * (opened_end == 0.0)[:, None, None]
    end_states = jnp.einsum(
        "ksgn,ksgep->kgenp", b_rows, inputs * outflow[..., None], precision=HIGH
    )
    start_states = jnp.einsum(
        "ksgn,ksgep->kgenp", c_rows, upstream * inflow[..., None], precision=HIGH
    )
    return (mixed_part, grad_part, inflow, outflow, through, end_states, start_states)


def block_terms(inputs, upstream, b_rows, c_rows, decay_rows, opened):

    def one_block(pieces):
        result = single_terms(*[piece[None] for piece in pieces])
        return tuple((item[0] for item in result))

    return lax.map(one_block, (inputs, upstream, b_rows, c_rows, decay_rows, opened))


def pass_forward(through, end_states, first_state):

    def advance(current, element):
        return (element[0][:, :, None, None] * current + element[1], current)

    final, entering = lax.scan(advance, first_state, (through, end_states))
    return (entering, final)


def pass_backward(through, start_states, last_state):

    def advance(current, element):
        return (element[0][:, :, None, None] * current + element[1], current)

    final, leaving = lax.scan(advance, last_state, (through, start_states), reverse=True)
    return (leaving, final)


def finish(terms, inputs, upstream, b_rows, c_rows, skip_gain, first_state, last_state):
    mixed_part, grad_part, inflow, outflow, through, end_states, start_states = terms
    entering, _ = pass_forward(through, end_states, first_state)
    leaving, _ = pass_backward(through, start_states, last_state)
    gain_wide = skip_gain[None, None, :, :, None]
    mixed = (
        mixed_part
        + jnp.einsum("ktgn,kgenp->ktgep", c_rows, entering, precision=HIGH) * inflow[..., None]
        + gain_wide * inputs
    )
    grads = (
        grad_part
        + jnp.einsum("ktgn,kgenp->ktgep", b_rows, leaving, precision=HIGH) * outflow[..., None]
        + gain_wide * upstream
    )
    return (mixed, grads)


def body(emitted, cotangent, b_proj, c_proj, log_decay, starts, skip):
    shifted = from_behind(emitted, "pipe", 1)
    inputs = jnp.where(lax.axis_index("pipe") == 0, emitted, shifted)[0]
    upstream = cotangent[0]
    length_dev = inputs.shape[0]
    local_heads = skip.shape[1]
    per_group = BLEND_CHANNELS // GROUPS
    seq_count = lax.axis_size("seq")
    head_share = local_heads // seq_count
    position = lax.axis_index("seq")
    flags = starts.astype(jnp.bfloat16)
    b_whole, c_whole, flag_whole = (
        lax.all_gather(b_proj, "seq", axis=1, tiled=True),
        lax.all_gather(c_proj, "seq", axis=1, tiled=True),
        lax.all_gather(flags, "seq", axis=1, tiled=True),
    )
    total_rows = length_dev * seq_count
    group_count = b_proj.shape[2] // N
    first_head = position * head_share
    group_pick = first_head // per_group
    b_rows = lax.dynamic_slice_in_dim(
        b_whole[0].reshape(total_rows, group_count, N), group_pick, 1, 1
    )
    c_rows = lax.dynamic_slice_in_dim(
        c_whole[0].reshape(total_rows, group_count, N), group_pick, 1, 1
    )
    outgoing = (
        inputs.reshape(length_dev, seq_count, head_share * P_SIZE),
        upstream.reshape(length_dev, seq_count, head_share * P_SIZE),
        log_decay[0].reshape(length_dev, seq_count, head_share),
    )
    got_inputs, got_upstream, got_decay = (
        lax.all_to_all(outgoing[0], "seq", split_axis=1, concat_axis=0, tiled=True),
        lax.all_to_all(outgoing[1], "seq", split_axis=1, concat_axis=0, tiled=True),
        lax.all_to_all(outgoing[2], "seq", split_axis=1, concat_axis=0, tiled=True),
    )
    block_count = total_rows // SPAN
    blocked = (block_count, SPAN, 1, head_share, P_SIZE)
    values = got_inputs.astype(jnp.float32).reshape(blocked)
    grads_in = got_upstream.astype(jnp.float32).reshape(blocked)
    b_blocks = b_rows.astype(jnp.float32).reshape(block_count, SPAN, 1, N)
    c_blocks = c_rows.astype(jnp.float32).reshape(block_count, SPAN, 1, N)
    decay_rows = got_decay.astype(jnp.float32).reshape(block_count, SPAN, 1, head_share)
    opened = flag_whole[0].astype(jnp.float32).reshape(block_count, SPAN)
    skip_gain = lax.dynamic_slice_in_dim(skip[0], first_head, head_share).reshape(1, head_share)
    terms = block_terms(values, grads_in, b_blocks, c_blocks, decay_rows, opened)
    empty_state = jnp.zeros((1, head_share, N, P_SIZE), jnp.float32)
    mixed, grads = finish(
        terms, values, grads_in, b_blocks, c_blocks, skip_gain, empty_state, empty_state
    )
    homeward = (
        mixed.reshape(total_rows, 1, head_share * P_SIZE).astype(jnp.bfloat16),
        grads.reshape(total_rows, 1, head_share * P_SIZE).astype(jnp.bfloat16),
    )
    mixed_back, grad_back = (
        lax.all_to_all(homeward[0], "seq", split_axis=0, concat_axis=1, tiled=True),
        lax.all_to_all(homeward[1], "seq", split_axis=0, concat_axis=1, tiled=True),
    )
    mixed_out = mixed_back.reshape(1, length_dev, local_heads * P_SIZE)
    grad_out = grad_back.reshape(1, length_dev, local_heads * P_SIZE)
    return (mixed_out, grad_out)


def solution(mesh):
    placed = (
        P("pipe", "seq", "tp"),
        P("pipe", "seq", "tp"),
        P("pipe", "seq", "tp"),
        P("pipe", "seq", "tp"),
        P("pipe", "seq", "tp"),
        P("pipe", "seq"),
        P("pipe", "tp"),
    )
    return jax.shard_map(
        body,
        mesh=mesh,
        in_specs=placed,
        out_specs=(P("pipe", "seq", "tp"), P("pipe", "seq", "tp")),
        check_vma=False,
    )
```

profile of v0, /device:TPU:0, one launch (start us, length us, event | category | flops | bytes accessed | tf_op | source)
XLA Modules:
  0.0 304.2 jit_solution(10501913095866550804)
XLA Ops:
  0.6 3.3 %collective-permute-start = (bf16[1,128,4096]{2,1,0:T(8,128)(2,1)}, bf16[1,128,4096]{2,1,0:T(8,128)(2,1)}, u32[]{:S(2)}, u32[]{:S(2)}) collective-permute-start(bf16[1,128,4096]{2,1,0:T(8,128)(2,1)} %param.13), channel_id=1, source_target_pairs={{0,8},{8,16},{16,24},{1,9},{9,17},{17,25},{2,10},{10,18},{18,26},{... | collective-permute-start | bytes 3145736 | tf_op jit(solution)/shard_map/ppermute | solution.py:19
  4.0 5.7 %all-to-all-start.1 = ((bf16[128,4,16]{0,2,1:T(8,128)(2,1)}), bf16[128,4,16]{0,2,1:T(8,128)(2,1)S(1)}, u32[]{:S(2)}, u32[]{:S(2)}) async-start(bf16[128,4,16]{0,2,1:T(8,128)(2,1)} %bitcast.249), calls=%async_computation.1 | async-start | bytes 32768 | tf_op jit(solution)/shard_map/all_to_all | solution.py:130
  12.0 3.3 %all-to-all-done.1 = bf16[128,4,16]{0,2,1:T(8,128)(2,1)S(1)} async-done(((bf16[128,4,16]{0,2,1:T(8,128)(2,1)}), bf16[128,4,16]{0,2,1:T(8,128)(2,1)S(1)}, u32[]{:S(2)}, u32[]{:S(2)}) %all-to-all-start.1) | async-done | bytes 16416 | tf_op jit(solution)/shard_map/all_to_all | solution.py:130
  15.3 3.5 %all-to-all-start.2 = ((bf16[128,4,1024]{0,2,1:T(8,128)(2,1)}), bf16[128,4,1024]{0,2,1:T(8,128)(2,1)S(1)}, u32[]{:S(2)}, u32[]{:S(2)}) async-start(bf16[128,4,1024]{0,2,1:T(8,128)(2,1)} %bitcast.36), calls=%async_computation.2 | async-start | bytes 2097152 | tf_op jit(solution)/shard_map/all_to_all | solution.py:129
  20.3 24.0 %all-to-all-done.2 = bf16[128,4,1024]{0,2,1:T(8,128)(2,1)S(1)} async-done(((bf16[128,4,1024]{0,2,1:T(8,128)(2,1)}), bf16[128,4,1024]{0,2,1:T(8,128)(2,1)S(1)}, u32[]{:S(2)}, u32[]{:S(2)}) %all-to-all-start.2) | async-done | bytes 1048608 | tf_op jit(solution)/shard_map/all_to_all | solution.py:129
  44.4 4.2 %all-to-all-start = ((bf16[128,4,1024]{0,2,1:T(8,128)(2,1)}), bf16[128,4,1024]{0,2,1:T(8,128)(2,1)}, u32[]{:S(2)}, u32[]{:S(2)}) async-start(bf16[128,4,1024]{0,2,1:T(8,128)(2,1)} %bitcast.25), calls=%async_computation | async-start | bytes 2097152 | tf_op jit(solution)/shard_map/all_to_all | solution.py:128
  48.8 32.7 %all_gather.10 = bf16[1,512,256]{2,1,0:T(8,128)(2,1)S(1)} all-gather(bf16[1,128,256]{2,1,0:T(8,128)(2,1)S(1)} %copy-done.6), channel_id=1, replica_groups=mesh['pipe'=4,'seq'=4,'tp'=2] {'seq'}, dimensions={1}, use_global_device_ids=true | all-gather | bytes 327680 | tf_op jit(solution)/shard_map/all_gather | solution.py:108
  82.2 14.3 %all_gather.11 = bf16[1,512,256]{2,1,0:T(8,128)(2,1)S(1)} all-gather(bf16[1,128,256]{2,1,0:T(8,128)(2,1)S(1)} %copy-done.7), channel_id=1, replica_groups=mesh['pipe'=4,'seq'=4,'tp'=2] {'seq'}, dimensions={1}, use_global_device_ids=true | all-gather | bytes 327680 | tf_op jit(solution)/shard_map/all_gather | solution.py:109
  100.3 9.9 %all_gather.9 = bf16[1,512]{1,0:T(2,128)(2,1)S(1)} all-gather(bf16[1,128]{1,0:T(2,128)(2,1)S(1)} %convert_element_type.127), channel_id=1, replica_groups=mesh['pipe'=4,'seq'=4,'tp'=2] {'seq'}, dimensions={1}, use_global_device_ids=true | all-gather | bytes 1280 | tf_op jit(solution)/shard_map/all_gather | solution.py:110
  113.2 2.8 bitcast_convert_fusion.1
  115.9 67.3 %while.52 = (s32[]{:T(128)}, f32[4,128,1,16,64]{1,4,3,2,0:T(8,128)}, f32[4,128,1,16,64]{1,4,3,2,0:T(8,128)}, f32[4,128,1,16]{3,2,1,0:T(1,128)}, f32[4,128,1,16]{...) while((s32[]{:T(128)}, ...), condition=%wide.region_3.4_spmd, body=%wide.region_0.3_spmd.sunk | while | flops 833169792 | bytes 5126091 | solution.py:57
  124.9 3.1 %fusion.92 = f32[4,128,1,16,64]{1,4,3,2,0:T(8,128)} fusion(f32[4,128,1,16,64]{1,4,3,2,0:T(8,128)} %get-tuple-element.615, s32[]{:T(128)} %get-tuple-element.613, f32[128,128]{1,0:T(8,128)S(1)} %copy.165, f32[128,16]{0,1:T(8,128)S(1)} %bitcast.244, pred[128,128]{1,0:T(8,128)(4,1)S(1)} %fusion.90, f32[4,128,1,16,64]{1,4,3,2,0:T(8,128)} %get-tuple-element.643), kind=kOutput, calls=%fused_computation.5.clone.1 | convolution fusion | flops 202375168 | bytes 1147904 | tf_op jit(solution)/shard_map/while/body/eval_jaxpr/ktsge,ktgep->ksgep/dot_general | solution.py:35
  128.0 4.1 %fusion.91 = f32[4,128,1,16,64]{1,4,3,2,0:T(8,128)} fusion(f32[4,128,1,16,64]{1,4,3,2,0:T(8,128)} %get-tuple-element.614, s32[]{:T(128)} %get-tuple-element.613, f32[128,128]{1,0:T(8,128)S(1)} %copy.165, f32[128,16]{0,1:T(8,128)S(1)} %bitcast.245, pred[128,128]{1,0:T(8,128)(4,1)S(1)} %fusion.90, f32[4,128,1,16,64]{1,4,3,2,0:T(8,128)} %get-tuple-element.638), kind=kOutput, calls=%fused_computation.7.clone.1 | convolution fusion | flops 202375168 | bytes 1147904 | tf_op jit(solution)/shard_map/while/body/eval_jaxpr/ktsge,ksgep->ktgep/dot_general | solution.py:34
  141.8 3.1 %fusion.92 = f32[4,128,1,16,64]{1,4,3,2,0:T(8,128)} fusion(f32[4,128,1,16,64]{1,4,3,2,0:T(8,128)} %get-tuple-element.615, s32[]{:T(128)} %get-tuple-element.613, f32[128,128]{1,0:T(8,128)S(1)} %copy.165, f32[128,16]{0,1:T(8,128)S(1)} %bitcast.244, pred[128,128]{1,0:T(8,128)(4,1)S(1)} %fusion.90, f32[4,128,1,16,64]{1,4,3,2,0:T(8,128)} %get-tuple-element.643), kind=kOutput, calls=%fused_computation.5.clone.1 | convolution fusion | flops 202375168 | bytes 1147904 | tf_op jit(solution)/shard_map/while/body/eval_jaxpr/ktsge,ktgep->ksgep/dot_general | solution.py:35
  144.9 4.1 %fusion.91 = f32[4,128,1,16,64]{1,4,3,2,0:T(8,128)} fusion(f32[4,128,1,16,64]{1,4,3,2,0:T(8,128)} %get-tuple-element.614, s32[]{:T(128)} %get-tuple-element.613, f32[128,128]{1,0:T(8,128)S(1)} %copy.165, f32[128,16]{0,1:T(8,128)S(1)} %bitcast.245, pred[128,128]{1,0:T(8,128)(4,1)S(1)} %fusion.90, f32[4,128,1,16,64]{1,4,3,2,0:T(8,128)} %get-tuple-element.638), kind=kOutput, calls=%fused_computation.7.clone.1 | convolution fusion | flops 202375168 | bytes 1147904 | tf_op jit(solution)/shard_map/while/body/eval_jaxpr/ktsge,ksgep->ktgep/dot_general | solution.py:34
  158.6 3.1 %fusion.92 = f32[4,128,1,16,64]{1,4,3,2,0:T(8,128)} fusion(f32[4,128,1,16,64]{1,4,3,2,0:T(8,128)} %get-tuple-element.615, s32[]{:T(128)} %get-tuple-element.613, f32[128,128]{1,0:T(8,128)S(1)} %copy.165, f32[128,16]{0,1:T(8,128)S(1)} %bitcast.244, pred[128,128]{1,0:T(8,128)(4,1)S(1)} %fusion.90, f32[4,128,1,16,64]{1,4,3,2,0:T(8,128)} %get-tuple-element.643), kind=kOutput, calls=%fused_computation.5.clone.1 | convolution fusion | flops 202375168 | bytes 1147904 | tf_op jit(solution)/shard_map/while/body/eval_jaxpr/ktsge,ktgep->ksgep/dot_general | solution.py:35
  161.7 4.0 %fusion.91 = f32[4,128,1,16,64]{1,4,3,2,0:T(8,128)} fusion(f32[4,128,1,16,64]{1,4,3,2,0:T(8,128)} %get-tuple-element.614, s32[]{:T(128)} %get-tuple-element.613, f32[128,128]{1,0:T(8,128)S(1)} %copy.165, f32[128,16]{0,1:T(8,128)S(1)} %bitcast.245, pred[128,128]{1,0:T(8,128)(4,1)S(1)} %fusion.90, f32[4,128,1,16,64]{1,4,3,2,0:T(8,128)} %get-tuple-element.638), kind=kOutput, calls=%fused_computation.7.clone.1 | convolution fusion | flops 202375168 | bytes 1147904 | tf_op jit(solution)/shard_map/while/body/eval_jaxpr/ktsge,ksgep->ktgep/dot_general | solution.py:34
  175.4 3.1 %fusion.92 = f32[4,128,1,16,64]{1,4,3,2,0:T(8,128)} fusion(f32[4,128,1,16,64]{1,4,3,2,0:T(8,128)} %get-tuple-element.615, s32[]{:T(128)} %get-tuple-element.613, f32[128,128]{1,0:T(8,128)S(1)} %copy.165, f32[128,16]{0,1:T(8,128)S(1)} %bitcast.244, pred[128,128]{1,0:T(8,128)(4,1)S(1)} %fusion.90, f32[4,128,1,16,64]{1,4,3,2,0:T(8,128)} %get-tuple-element.643), kind=kOutput, calls=%fused_computation.5.clone.1 | convolution fusion | flops 202375168 | bytes 1147904 | tf_op jit(solution)/shard_map/while/body/eval_jaxpr/ktsge,ktgep->ksgep/dot_general | solution.py:35
  178.5 4.1 %fusion.91 = f32[4,128,1,16,64]{1,4,3,2,0:T(8,128)} fusion(f32[4,128,1,16,64]{1,4,3,2,0:T(8,128)} %get-tuple-element.614, s32[]{:T(128)} %get-tuple-element.613, f32[128,128]{1,0:T(8,128)S(1)} %copy.165, f32[128,16]{0,1:T(8,128)S(1)} %bitcast.245, pred[128,128]{1,0:T(8,128)(4,1)S(1)} %fusion.90, f32[4,128,1,16,64]{1,4,3,2,0:T(8,128)} %get-tuple-element.638), kind=kOutput, calls=%fused_computation.7.clone.1 | convolution fusion | flops 202375168 | bytes 1147904 | tf_op jit(solution)/shard_map/while/body/eval_jaxpr/ktsge,ksgep->ktgep/dot_general | solution.py:34
  185.8 18.4 %while.54 = (s32[]{:T(128)}, f32[1,16,128,64]{3,2,1,0:T(8,128)S(1)}, f32[4,1,16,128,64]{4,3,2,1,0:T(8,128)}, f32[4,1,16]{2,1,0:T(1,128)S(1)}, f32[4,1,16,128,64]...) while((s32[]{:T(128)}, f32[1,16,128,64]{3,2,1,0:T(8,128)S(1)}, ...), condition=%wide.region_7.8_spmd.clone, body=%wide.region_6.7_spmd.clone.sunk | while | flops 524292 | bytes 5243192 | solution.py:74
  205.2 6.9 %fusion.50 = bf16[4,128,1,16,64]{1,4,3,0,2:T(8,128)(2,1)S(1)} fusion(f32[4,128,1,16,64]{1,4,3,2,0:T(8,128)} %get-tuple-element.215, f32[4,128,1,16,64]{1,4,3,0,2:T(8,128)} %bitcast.235, bf16[4,128,128,1]{2,1,3,0:T(8,128)(2,1)S(1)} %bitcast.243, f32[4,1,16,128,64]{4,3,2,1,0:T(8,128)} %get-tuple-element.217, f32[4,128,16]{1,2,0:T(8,128)S(1)} %copy.136, ...), kind=kOutput, calls=%fused_computation.76 | convolution fusion | flops 807927808 | bytes 7503936 | tf_op jit(solution)/shard_map/ktgn,kgenp->ktgep/dot_general | solution.py:90
  212.1 2.5 copy.150
  214.6 8.0 %reshape.498 = bf16[512,1,1024]{2,1,0:T(2,128)(2,1)} reshape(bf16[4,128,1,16,64]{4,3,1,0,2:T(8,128)(2,1)} %copy.150) | data formatting | bytes 2097152 | tf_op jit(solution)/shard_map/convert_element_type | solution.py:148
  223.2 8.1 %reduce.1 = bf16[512,1024]{1,0:T(8,128)(2,1)S(1)} reduce(bf16[512,1,1024]{2,1,0:T(2,128)(2,1)} %reshape.498, bf16[]{:T(256)} %broadcast.237), dimensions={1}, to_apply=%reshape.498.reduce_sub_computation | reduce | bytes 2097154 | tf_op jit(solution)/shard_map/convert_element_type | solution.py:148
  233.3 4.2 %all-to-all-start.4 = ((bf16[4,2,65536]{2,1,0:T(2,128)(2,1)}), bf16[4,2,65536]{2,1,0:T(2,128)(2,1)}, u32[]{:S(2)}, u32[]{:S(2)}) async-start(bf16[4,2,65536]{2,1,0:T(2,128)(2,1)} %reshape.501), calls=%async_computation.4 | async-start | bytes 2097152 | tf_op jit(solution)/shard_map/all_to_all | solution.py:152
  240.0 11.0 %while.53 = (s32[]{:T(128)}, f32[1,16,128,64]{3,2,1,0:T(8,128)S(1)}, f32[4,1,16,128,64]{4,3,2,1,0:T(8,128)}, f32[4,1,16]{2,1,0:T(1,128)S(1)}, f32[4,1,16,128,64]{3,4,2,1,0:T(8,128)}, /*index=5*/s32[]{:T(128)}, s32[]{:T(128)}) while((s32[]{:T(128)}, f32[1,16,128,64]{3,2,1,0:T(8,128)S(1)}, f32[4,1,16,128,64]{4,3,2,1,0:T(8,128)}, ...), condition=%wide.region_5.6_spmd.clone, body=%wide.region_4.5_spmd.clone.sunk | while | flops 524291 | bytes 5243680 | solution.py:65
  251.1 6.9 %fusion.53 = bf16[4,128,1,16,64]{1,4,3,0,2:T(8,128)(2,1)S(1)} fusion(f32[4,128,1,16,64]{1,4,3,2,0:T(8,128)} %get-tuple-element.210, f32[4,128,1,16,64]{1,4,3,0,2:T(8,128)} %bitcast.233, bf16[4,128,128,1]{2,1,3,0:T(8,128)(2,1)S(1)} %bitcast.241, f32[4,1,16,128,64]{4,3,2,1,0:T(8,128)} %get-tuple-element.213, f32[16]{0:T(128)S(1)} %fusion.58, ...), kind=kOutput, calls=%fused_computation.80 | convolution fusion | flops 807927808 | bytes 7503936 | tf_op jit(solution)/shard_map/ktgn,kgenp->ktgep/dot_general | solution.py:85
  260.6 7.0 %reshape.497 = bf16[512,1,1024]{2,1,0:T(2,128)(2,1)S(1)} reshape(bf16[4,128,1,16,64]{4,3,1,0,2:T(8,128)(2,1)} %copy.149) | data formatting | bytes 2097152 | tf_op jit(solution)/shard_map/convert_element_type | solution.py:147
  267.5 7.3 %reduce = bf16[512,1024]{1,0:T(8,128)(2,1)S(1)} reduce(bf16[512,1,1024]{2,1,0:T(2,128)(2,1)S(1)} %reshape.497, bf16[]{:T(256)} %broadcast.237), dimensions={1}, to_apply=%reshape.497.reduce_sub_computation | reduce | bytes 2097154 | tf_op jit(solution)/shard_map/convert_element_type | solution.py:147
  276.9 5.0 %all-to-all-start.3 = ((bf16[4,2,65536]{2,1,0:T(2,128)(2,1)}), bf16[4,2,65536]{2,1,0:T(2,128)(2,1)S(1)}, u32[]{:S(2)}, u32[]{:S(2)}) async-start(bf16[4,2,65536]{2,1,0:T(2,128)(2,1)} %reshape.499), calls=%async_computation.3 | async-start | bytes 2097152 | tf_op jit(solution)/shard_map/all_to_all | solution.py:151
  281.9 2.6 reshape.502
  288.8 12.0 %all-to-all-done.3 = bf16[4,2,65536]{2,1,0:T(2,128)(2,1)S(1)} async-done(((bf16[4,2,65536]{2,1,0:T(2,128)(2,1)}), bf16[4,2,65536]{2,1,0:T(2,128)(2,1)S(1)}, u32[]{:S(2)}, u32[]{:S(2)}) %all-to-all-start.3) | async-done | bytes 1048608 | tf_op jit(solution)/shard_map/all_to_all | solution.py:151
  (170 shorter events, 96.9 us)
Async XLA Ops:
  0.6 109.6 %copy-start = (f32[1,64]{1,0:T(1,128)S(1)}, f32[1,64]{1,0:T(1,128)}, u32[]{:S(2)}) copy-start(f32[1,64]{1,0:T(1,128)} %param.19) | copy-start | bytes 772
  0.6 18.2 %collective-permute-start = (bf16[1,128,4096]{2,1,0:T(8,128)(2,1)}, bf16[1,128,4096]{2,1,0:T(8,128)(2,1)}, u32[]{:S(2)}, u32[]{:S(2)}) collective-permute-start(bf16[1,128,4096]{2,1,0:T(8,128)(2,1)} %param.13), channel_id=1, source_target_pairs={{0,8},{8,16},{16,24},{1,9},{9,17},{17,25},{2,10},{10,18},{18,26},{... | collective-permute-start | bytes 3145736 | tf_op jit(solution)/shard_map/ppermute | solution.py:19
  4.0 11.3 %all-to-all-start.1 = ((bf16[128,4,16]{0,2,1:T(8,128)(2,1)}), bf16[128,4,16]{0,2,1:T(8,128)(2,1)S(1)}, u32[]{:S(2)}, u32[]{:S(2)}) async-start(bf16[128,4,16]{0,2,1:T(8,128)(2,1)} %bitcast.249), calls=%async_computation.1 | async-start | bytes 32768 | tf_op jit(solution)/shard_map/all_to_all | solution.py:130
  9.7 9.2 %copy-start.4 = (bf16[1,128,4096]{2,1,0:T(8,128)(2,1)S(1)}, bf16[1,128,4096]{2,1,0:T(8,128)(2,1)}, u32[]{:S(2)}) copy-start(bf16[1,128,4096]{2,1,0:T(8,128)(2,1)} %param.13) | copy-start | bytes 3145732
  15.3 3.5 %copy-start.8 = (bf16[128,4,16]{0,2,1:T(8,128)(2,1)}, bf16[128,4,16]{0,2,1:T(8,128)(2,1)S(1)}, u32[]{:S(2)}) copy-start(bf16[128,4,16]{0,2,1:T(8,128)(2,1)S(1)} %all-to-all-done.1) | copy-start | bytes 49156
  15.3 29.1 %all-to-all-start.2 = ((bf16[128,4,1024]{0,2,1:T(8,128)(2,1)}), bf16[128,4,1024]{0,2,1:T(8,128)(2,1)S(1)}, u32[]{:S(2)}, u32[]{:S(2)}) async-start(bf16[128,4,1024]{0,2,1:T(8,128)(2,1)} %bitcast.36), calls=%async_computation.2 | async-start | bytes 2097152 | tf_op jit(solution)/shard_map/all_to_all | solution.py:129
  19.0 29.7 %copy-start.6 = (bf16[1,128,256]{2,1,0:T(8,128)(2,1)S(1)}, bf16[1,128,256]{2,1,0:T(8,128)(2,1)}, u32[]{:S(2)}) copy-start(bf16[1,128,256]{2,1,0:T(8,128)(2,1)} %param.15) | copy-start | bytes 196612
  19.0 63.2 %copy-start.7 = (bf16[1,128,256]{2,1,0:T(8,128)(2,1)S(1)}, bf16[1,128,256]{2,1,0:T(8,128)(2,1)}, u32[]{:S(2)}) copy-start(bf16[1,128,256]{2,1,0:T(8,128)(2,1)} %param.16) | copy-start | bytes 196612
  44.4 68.8 %all-to-all-start = ((bf16[128,4,1024]{0,2,1:T(8,128)(2,1)}), bf16[128,4,1024]{0,2,1:T(8,128)(2,1)}, u32[]{:S(2)}, u32[]{:S(2)}) async-start(bf16[128,4,1024]{0,2,1:T(8,128)(2,1)} %bitcast.25), calls=%async_computation | async-start | bytes 2097152 | tf_op jit(solution)/shard_map/all_to_all | solution.py:128
  48.7 51.6 %copy-start.9 = (s32[1,128]{1,0:T(1,128)S(1)}, s32[1,128]{1,0:T(1,128)}, u32[]{:S(2)}) copy-start(s32[1,128]{1,0:T(1,128)} %param.18) | copy-start | bytes 1540
  98.9 0.7 copy-start.2
  113.2 2.8 copy-start.1
  185.8 19.4 %copy-start.3 = (bf16[512,1,128]{2,0,1:T(8,128)(2,1)S(1)}, bf16[512,1,128]{2,0,1:T(8,128)(2,1)}, u32[]{:S(2)}) copy-start(bf16[512,1,128]{2,0,1:T(8,128)(2,1)} %copy-done.2) | copy-start | bytes 393220
  233.3 43.6 %all-to-all-start.4 = ((bf16[4,2,65536]{2,1,0:T(2,128)(2,1)}), bf16[4,2,65536]{2,1,0:T(2,128)(2,1)}, u32[]{:S(2)}, u32[]{:S(2)}) async-start(bf16[4,2,65536]{2,1,0:T(2,128)(2,1)} %reshape.501), calls=%async_computation.4 | async-start | bytes 2097152 | tf_op jit(solution)/shard_map/all_to_all | solution.py:152
  240.0 11.0 %copy-start.5 = (f32[4,128,1,16]{3,2,1,0:T(1,128)S(1)}, f32[4,128,1,16]{3,2,1,0:T(1,128)}, u32[]{:S(2)}) copy-start(f32[4,128,1,16]{3,2,1,0:T(1,128)} %get-tuple-element.214) | copy-start | bytes 98308
  276.9 24.0 %all-to-all-start.3 = ((bf16[4,2,65536]{2,1,0:T(2,128)(2,1)}), bf16[4,2,65536]{2,1,0:T(2,128)(2,1)S(1)}, u32[]{:S(2)}, u32[]{:S(2)}) async-start(bf16[4,2,65536]{2,1,0:T(2,128)(2,1)} %reshape.499), calls=%async_computation.3 | async-start | bytes 2097152 | tf_op jit(solution)/shard_map/all_to_all | solution.py:151
where the time goes:
time: 307 us; the launch traced here: 304 us
  local copies, waits for them, and re-layouts  73.4 us (24%)
  matrix products  63.1 us (21%)
  blocking collectives  56.9 us (19%)
  other arithmetic  41.3 us (13%)
  waiting for transfers between devices  39.3 us (13%)
  starting transfers between devices  26.1 us (9%)
  loops' own time  3.11 us (1%)
    all_gather x1, blocking collectives, body(): lax.all_gather(b_proj, 'seq', axis=1, tiled=True)  32.7 us
    all_to_all x1, waiting for transfers between devices, body(): lax.all_to_all(outgoing[1], 'seq', split_axis=1, concat_axis=0, tiled=True)  24 us
    dynamic_slice x16, local copies, waits for them, and re-layouts, pass_forward(): final, entering = lax.scan(advance, first_state, (through, end_states))  18.7 us
    dot_general x4, matrix products, single_terms(): jnp.einsum('ktsge,ksgep->ktgep', mixing, inputs, precision=HIGH)  16.2 us
    all_gather x1, blocking collectives, body(): lax.all_gather(c_proj, 'seq', axis=1, tiled=True)  14.3 us
    dynamic_update_slice x16, other arithmetic, block_terms(): lax.map(one_block, (inputs, upstream, b_rows, c_rows, decay_rows, opened))  12.7 us
    unnamed x30, local copies, waits for them, and re-layouts  12.6 us
    dot_general x4, matrix products, single_terms(): jnp.einsum('ktsge,ktgep->ksgep', mixing, upstream, precision=HIGH)  12.5 us
  transfers between devices with their start and end apart: 6, of which 3 were waited for; matrix products, arithmetic and copies ran while one was open for 19% of the time, Pallas kernels for 0%

commit v1 on v0

v1 whole, which is shorter than its diff:
```python
import functools

import jax
import jax.numpy as jnp
from jax import lax
from jax.experimental import pallas as pl
from jax.experimental.pallas import tpu as pltpu
from jax.sharding import PartitionSpec as P

BLEND_CHANNELS = 128
P_SIZE = 64
N = 128
GROUPS = 4
COLS = 512
MESH = pl.DeviceIdType.MESH
F32 = jnp.float32
BF16 = jnp.bfloat16


def split(value):
    high = value.astype(BF16)
    return high, (value - high.astype(F32)).astype(BF16)


def dot(a, b):
    return jnp.dot(a, b, preferred_element_type=F32)


def kernel(
    pipe_count, seq_count, cols,
    e_ref, g_ref, b_ref, c_ref, d_ref, st_ref, sk_ref,
    mixed_ref, grad_ref,
    x_buf, up_out, up_in, down_out, down_in,
    small, centre, lhs_up, lhs_down, low_up, low_down, enter_up, enter_down,
    part_up, part_down, own_up, own_down, gone_row,
    x_send, x_recv, up_send, up_recv, down_send, down_recv,
):
    length = e_ref.shape[1]
    chunks = e_ref.shape[2] // cols
    heads = sk_ref.shape[1]
    group_count = b_ref.shape[2] // N
    chunk_heads = cols // P_SIZE
    chunks_per_group = chunks // group_count
    middle = length // 2 - 1
    pipe = lax.axis_index("pipe")
    seq = lax.axis_index("seq")
    has_prev_pipe, has_next_pipe = pipe > 0, pipe < pipe_count - 1
    has_prev, has_next = seq > 0, seq < seq_count - 1

    barrier = pltpu.get_barrier_semaphore()

    def greet(present, where):
        @pl.when(present)
        def _():
            pl.semaphore_signal(barrier, inc=1, device_id=where, device_id_type=MESH)

    greet(has_prev_pipe, {"pipe": pipe - 1})
    greet(has_next_pipe, {"pipe": pipe + 1})
    greet(has_prev, {"seq": seq - 1})
    greet(has_next, {"seq": seq + 1})
    count = (
        has_prev_pipe.astype(jnp.int32) + has_next_pipe.astype(jnp.int32)
        + has_prev.astype(jnp.int32) + has_next.astype(jnp.int32)
    )
    pl.semaphore_wait(barrier, count)

    def x_copy(j):
        return pltpu.make_async_remote_copy(
            src_ref=e_ref.at[0, :, pl.ds(pl.multiple_of(j * cols, cols), cols)],
            dst_ref=x_buf.at[j],
            send_sem=x_send.at[j], recv_sem=x_recv.at[j],
            device_id={"pipe": pipe + 1}, device_id_type=MESH,
        )

    def up_copy(j):
        return pltpu.make_async_remote_copy(
            src_ref=up_out.at[j], dst_ref=up_in.at[j],
            send_sem=up_send.at[j], recv_sem=up_recv.at[j],
            device_id={"seq": seq + 1}, device_id_type=MESH,
        )

    def down_copy(j):
        return pltpu.make_async_remote_copy(
            src_ref=down_out.at[j], dst_ref=down_in.at[j],
            send_sem=down_send.at[j], recv_sem=down_recv.at[j],
            device_id={"seq": seq - 1}, device_id_type=MESH,
        )

    @pl.when(has_next_pipe)
    def _():
        @pl.loop(0, chunks)
        def _(j):
            x_copy(j).start()

    row = lax.broadcasted_iota(jnp.int32, (length, length), 0)
    col = lax.broadcasted_iota(jnp.int32, (length, length), 1)
    starts_row = st_ref[...].astype(F32)
    starts_col = jnp.sum(jnp.where(row == col, starts_row, 0.0), axis=1, keepdims=True)
    opened_col = jnp.sum(jnp.where(col <= row, starts_row, 0.0), axis=1, keepdims=True)
    opened_row = jnp.sum(jnp.where(row <= col, starts_col, 0.0), axis=0, keepdims=True)
    opened_end = jnp.sum(starts_row, axis=1, keepdims=True)
    same = opened_col == opened_row
    link_up = jnp.logical_and(same, col <= row)
    link_down = jnp.logical_and(same, row <= col)
    in_mask = jnp.where(opened_col == 0.0, 1.0, 0.0)
    out_mask = jnp.where(opened_col == opened_end, 1.0, 0.0)
    gone_row[...] = jnp.broadcast_to(jnp.where(opened_end == 0.0, 1.0, 0.0), gone_row.shape)
    centre[...] = (
        jnp.where(col <= row, 1.0, 0.0) - jnp.where(col <= middle, 1.0, 0.0)
    ).astype(BF16)
    small[0:length, :] = d_ref[0]
    gain = sk_ref[...]
    gain_high = gain.astype(BF16).astype(F32)
    gain_mid = (gain - gain_high).astype(BF16).astype(F32)
    gain_low = gain - gain_high - gain_mid
    gain_row = lax.broadcasted_iota(jnp.int32, (16, heads), 0)
    small[length:, :] = jnp.where(
        gain_row == 0, gain_high,
        jnp.where(gain_row == 1, gain_mid, jnp.where(gain_row == 2, gain_low, 0.0)),
    ).astype(BF16)
    for q in range(group_count):
        b = b_ref[0, :, q * N:(q + 1) * N]
        c = c_ref[0, :, q * N:(q + 1) * N]
        contract = (((1,), (1,)), ((), ()))
        cross_up = lax.dot_general(c, b, contract, preferred_element_type=F32)
        cross_down = lax.dot_general(b, c, contract, preferred_element_type=F32)
        high, low = split(jnp.where(link_up, cross_up, 0.0))
        lhs_up[q, 0:length, 0:length] = high
        lhs_up[q, 0:length, length:] = high
        low_up[q] = low
        high, low = split(jnp.where(link_down, cross_down, 0.0))
        lhs_down[q, 0:length, 0:length] = high
        lhs_down[q, 0:length, length:] = high
        low_down[q] = low
        b_kept = b.astype(F32) * out_mask
        c_kept = c.astype(F32) * in_mask
        b_turned = b_kept.T.astype(BF16)
        c_turned = c_kept.T.astype(BF16)
        lhs_up[q, length:, 0:length] = b_turned
        lhs_up[q, length:, length:] = b_turned
        lhs_down[q, length:, 0:length] = c_turned
        lhs_down[q, length:, length:] = c_turned
        enter_up[q, :, 0:N] = c_kept.astype(BF16)
        enter_up[q, :, N:] = c_kept.astype(BF16)
        enter_down[q, :, 0:N] = b_kept.astype(BF16)
        enter_down[q, :, N:] = b_kept.astype(BF16)

    def factors(j):
        own = lax.broadcasted_iota(jnp.int32, (heads, cols), 0)
        lane = lax.broadcasted_iota(jnp.int32, (heads, cols), 1)
        first = own * P_SIZE - j * cols
        pick = jnp.logical_and(lane >= first, lane < first + P_SIZE)
        wide = dot(small[...], jnp.where(pick, 1.0, 0.0).astype(BF16))
        decay = wide[0:length]
        gain_wide = jnp.sum(wide[length:], axis=0, keepdims=True)
        shift = dot(centre[...], decay.astype(BF16))
        half = decay[0:1] - shift[0:1]
        return shift, half, gain_wide

    steps = chunks + seq_count - 1

    @pl.loop(0, steps)
    def _(step):
        ju = step - seq
        jd = step - (seq_count - 1 - seq)
        up_on = jnp.logical_and(ju >= 0, ju < chunks)
        down_on = jnp.logical_and(jd >= 0, jd < chunks)

        @pl.when(down_on)
        def _():
            q = jd // chunks_per_group
            shift, half, gain_wide = factors(jd)
            g = g_ref[0, :, pl.ds(pl.multiple_of(jd * cols, cols), cols)].astype(F32)
            high, low = split(g * jnp.exp(shift))
            both = dot(lhs_down[q], jnp.concatenate([high, low], axis=0))
            back = jnp.exp(-shift)
            part_down[0] = (both[0:length] + dot(low_down[q], high)) * back + gain_wide * g
            part_down[1] = back * jnp.exp(shift[length - 1:])
            own_down[0:N] = both[length:] * jnp.exp(half)
            own_down[N:N + 8] = jnp.broadcast_to(
                jnp.exp(half + shift[length - 1:]) * gone_row[0:1, 0:1], (8, cols)
            )

            @pl.when(seq == seq_count - 1)
            def _():
                down_in[jd] = jnp.zeros(down_in.shape[1:], BF16)

        @pl.when(up_on)
        def _():
            q = ju // chunks_per_group

            @pl.when(pipe == 0)
            def _():
                x_buf[ju] = e_ref[0, :, pl.ds(pl.multiple_of(ju * cols, cols), cols)]

            @pl.when(has_prev_pipe)
            def _():
                x_copy(ju).wait_recv()

            shift, half, gain_wide = factors(ju)
            x = x_buf[ju].astype(F32)
            high, low = split(x * jnp.exp(-shift))
            both = dot(lhs_up[q], jnp.concatenate([high, low], axis=0))
            forth = jnp.exp(shift)
            part_up[0] = (both[0:length] + dot(low_up[q], high)) * forth + gain_wide * x
            part_up[1] = forth * jnp.exp(half)
            own_up[0:N] = both[length:] * jnp.exp(shift[length - 1:])
            own_up[N:N + 8] = jnp.broadcast_to(
                jnp.exp(half + shift[length - 1:]) * gone_row[0:1, 0:1], (8, cols)
            )

            @pl.when(seq == 0)
            def _():
                up_in[ju] = jnp.zeros(up_in.shape[1:], BF16)

        @pl.when(jnp.logical_and(down_on, has_next))
        def _():
            down_copy(jd).wait_recv()

        @pl.when(jnp.logical_and(down_on, has_prev))
        def _():
            got = down_in[jd, 0:N].astype(F32) + down_in[jd, N:].astype(F32)
            high, low = split(got * own_down[N:N + 1] + own_down[0:N])
            down_out[jd, 0:N] = high
            down_out[jd, N:] = low
            down_copy(jd).start()

        @pl.when(jnp.logical_and(up_on, has_prev))
        def _():
            up_copy(ju).wait_recv()

        @pl.when(jnp.logical_and(up_on, has_next))
        def _():
            got = up_in[ju, 0:N].astype(F32) + up_in[ju, N:].astype(F32)
            high, low = split(got * own_up[N:N + 1] + own_up[0:N])
            up_out[ju, 0:N] = high
            up_out[ju, N:] = low
            up_copy(ju).start()

        @pl.when(down_on)
        def _():
            q = jd // chunks_per_group
            total = part_down[0] + dot(enter_down[q], down_in[jd]) * part_down[1]
            grad_ref[0, :, pl.ds(pl.multiple_of(jd * cols, cols), cols)] = total.astype(BF16)

        @pl.when(up_on)
        def _():
            q = ju // chunks_per_group
            total = part_up[0] + dot(enter_up[q], up_in[ju]) * part_up[1]
            mixed_ref[0, :, pl.ds(pl.multiple_of(ju * cols, cols), cols)] = total.astype(BF16)

    @pl.loop(0, chunks)
    def _(j):
        @pl.when(has_next_pipe)
        def _():
            x_copy(j).wait_send()

        @pl.when(has_next)
        def _():
            up_copy(j).wait_send()

        @pl.when(has_prev)
        def _():
            down_copy(j).wait_send()


def body(pipe_count, seq_count, emitted, cotangent, b_proj, c_proj, log_decay, starts, skip):
    _, length, width = emitted.shape
    heads = skip.shape[1]
    group_count = b_proj.shape[2] // N
    cols = COLS
    chunks = width // cols
    whole = pl.BlockSpec(memory_space=pltpu.VMEM)
    dma = pltpu.SemaphoreType.DMA
    return pl.pallas_call(
        functools.partial(kernel, pipe_count, seq_count, cols),
        out_shape=(
            jax.ShapeDtypeStruct(emitted.shape, BF16),
            jax.ShapeDtypeStruct(emitted.shape, BF16),
        ),
        in_specs=[whole] * 7,
        out_specs=(whole, whole),
        scratch_shapes=[
            pltpu.VMEM((chunks, length, cols), BF16),
            pltpu.VMEM((chunks, 2 * N, cols), BF16),
            pltpu.VMEM((chunks, 2 * N, cols), BF16),
            pltpu.VMEM((chunks, 2 * N, cols), BF16),
            pltpu.VMEM((chunks, 2 * N, cols), BF16),
            pltpu.VMEM((length + 16, heads), BF16),
            pltpu.VMEM((length, length), BF16),
            pltpu.VMEM((group_count, length + N, 2 * length), BF16),
            pltpu.VMEM((group_count, length + N, 2 * length), BF16),
            pltpu.VMEM((group_count, length, length), BF16),
            pltpu.VMEM((group_count, length, length), BF16),
            pltpu.VMEM((group_count, length, 2 * N), BF16),
            pltpu.VMEM((group_count, length, 2 * N), BF16),
            pltpu.VMEM((2, length, cols), F32),
            pltpu.VMEM((2, length, cols), F32),
            pltpu.VMEM((N + 8, cols), F32),
            pltpu.VMEM((N + 8, cols), F32),
            pltpu.VMEM((8, 128), F32),
            dma((chunks,)), dma((chunks,)), dma((chunks,)),
            dma((chunks,)), dma((chunks,)), dma((chunks,)),
        ],
        compiler_params=pltpu.CompilerParams(
            collective_id=0, has_side_effects=True, vmem_limit_bytes=40 * 1024 * 1024
        ),
    )(emitted, cotangent, b_proj, c_proj, log_decay, starts, skip)


def solution(mesh):
    wide = P("pipe", "seq", "tp")
    return jax.shard_map(
        functools.partial(body, mesh.shape["pipe"], mesh.shape["seq"]),
        mesh=mesh,
        in_specs=(wide, wide, wide, wide, wide, P("pipe", "seq"), P("pipe", "tp")),
        out_specs=(wide, wide),
        check_vma=False,
    )
```

time: 307 us -> 76.6 us (0.25)
  Pallas kernels: 0 us -> 68.3 us
  local copies, waits for them, and re-layouts: 73.4 us -> 6.91 us
  matrix products: 63.1 us -> 0 us
  blocking collectives: 56.9 us -> 0 us
  other arithmetic: 41.3 us -> 0 us
  waiting for transfers between devices: 39.3 us -> 0 us
  starting transfers between devices: 26.1 us -> 0 us
  loops' own time: 3.11 us -> 0 us
    pallas_call x0 -> x1, Pallas kernels: none -> 68.3 us  [body(): pl.pallas_call(functools.partial(kernel, pipe_count, seq_count, cols), ou...]
    dot_general x22 -> x0, matrix products: 63.1 us -> none  [the longest x4 16.2 us: single_terms(): jnp.einsum('ktsge,ksgep->ktgep', mixing, inputs, precision=HIGH)]
    all_gather x3 -> x0, blocking collectives: 56.9 us -> none  [the longest x1 32.7 us: body(): lax.all_gather(b_proj, 'seq', axis=1, tiled=True)]
    all_to_all x5 -> x0, waiting for transfers between devices: 39.3 us -> none  [the longest x1 24 us: body(): lax.all_to_all(outgoing[1], 'seq', split_axis=1, concat_axis=0, tiled=True)]
    convert_element_type x11 -> x0, other arithmetic: 23.6 us -> none  [the longest x1 8.07 us: body(): grads.reshape(total_rows, 1, head_share * P_SIZE).astype(jnp.bfloat16)]
    dynamic_slice x29 -> x0, local copies, waits for them, and re-layouts: 23.5 us -> none  [the longest x16 18.7 us: pass_forward(): final, entering = lax.scan(advance, first_state, (through, end_states))]
    all_to_all x5 -> x0, starting transfers between devices: 22.7 us -> none  [the longest x1 5.7 us: body(): lax.all_to_all(outgoing[2], 'seq', split_axis=1, concat_axis=0, tiled=True)]
    convert_element_type x5 -> x0, local copies, waits for them, and re-layouts: 20.6 us -> none  [the longest x2 10.5 us: body(): grads.reshape(total_rows, 1, head_share * P_SIZE).astype(jnp.bfloat16)]
  transfers between devices with their start and end apart: 6 -> 0, of which waited for: 3 -> 0; matrix products, arithmetic and copies ran while one was open for 19% -> 0% of each run, Pallas kernels for 0% -> 0%
where the time goes in v1:
time: 76.6 us; the launch traced here: 75.9 us
  Pallas kernels  68.3 us (89%)
  local copies, waits for them, and re-layouts  6.91 us (9%)
    pallas_call x1, Pallas kernels, body(): pl.pallas_call(functools.partial(kernel, pipe_count, seq_count, cols), ou...  68.3 us
    unnamed x15, local copies, waits for them, and re-layouts  6.91 us

profile of v1, /device:TPU:0, one launch (start us, length us, event | category | flops | bytes accessed | tf_op | source)
XLA Modules:
  0.0 75.9 jit_solution(12830036239393163775)
XLA Ops:
  0.6 0.0 copy-start.5
  0.6 0.0 copy-start.4
  0.7 0.8 %copy.9.d_ref = bf16[1,128,64]{2,1,0:T(8,128)(2,1)S(1)} copy(bf16[1,128,64]{1,2,0:T(8,128)(2,1)} %param.11) | data formatting | bytes 32768 | tf_op args[4]
  1.5 0.0 copy-done.5
  1.5 0.0 copy-done.4
  1.5 0.0 copy-start
  1.5 1.2 %copy-done = bf16[1,128,4096]{2,1,0:T(8,128)(2,1)S(1)} copy-done((bf16[1,128,4096]{2,1,0:T(8,128)(2,1)S(1)}, bf16[1,128,4096]{2,1,0:T(8,128)(2,1)}, u32[]{:S(2)}) %copy-start) | copy-done | bytes 1048600
  2.7 0.0 copy-start.1
  2.7 1.2 %copy-done.1 = bf16[1,128,4096]{2,1,0:T(8,128)(2,1)S(1)} copy-done((bf16[1,128,4096]{2,1,0:T(8,128)(2,1)S(1)}, bf16[1,128,4096]{2,1,0:T(8,128)(2,1)}, u32[]{:S(2)}) %copy-start.1) | copy-done | bytes 1048600
  4.0 0.0 copy-start.2
  4.0 0.8 %copy-done.2 = bf16[1,128,256]{2,1,0:T(8,128)(2,1)S(1)} copy-done((bf16[1,128,256]{2,1,0:T(8,128)(2,1)S(1)}, bf16[1,128,256]{2,1,0:T(8,128)(2,1)}, u32[]{:S(2)}) %copy-start.2) | copy-done | bytes 65560
  4.8 0.0 copy-start.3
  4.8 0.8 %copy-done.3 = bf16[1,128,256]{2,1,0:T(8,128)(2,1)S(1)} copy-done((bf16[1,128,256]{2,1,0:T(8,128)(2,1)S(1)}, bf16[1,128,256]{2,1,0:T(8,128)(2,1)}, u32[]{:S(2)}) %copy-start.3) | copy-done | bytes 65560
  5.6 68.3 %shard_map.86 = (bf16[1,128,4096]{2,1,0:T(8,128)(2,1)S(1)}, bf16[1,128,4096]{2,1,0:T(8,128)(2,1)S(1)}) custom-call(bf16[1,128,4096]{2,1,0:T(8,128)(2,1)S(1)} %copy-done, bf16[1,128,4096]{2,1,0:T(8,128)(2,1)S(1)} %copy-done.1, bf16[1,128,256]{2,1,0:T(8,128)(2,1)S(1)} %copy-done.2, bf16[1,128,256]{2,1,0:T(8,128)(2,1)S(1)} %copy-done.3, ...), custom_call_target="tpu_custom_call" | custom-call | tf_op jit(solution)/shard_map/pallas_call | solution.py:275
  74.0 1.0 %copy.12 = bf16[1,128,4096]{2,1,0:T(8,128)(2,1)} copy(bf16[1,128,4096]{2,1,0:T(8,128)(2,1)S(1)} %get-tuple-element.4) | data formatting | bytes 2097152
  74.9 1.0 %copy.13 = bf16[1,128,4096]{2,1,0:T(8,128)(2,1)} copy(bf16[1,128,4096]{2,1,0:T(8,128)(2,1)S(1)} %get-tuple-element.5) | data formatting | bytes 2097152
Async XLA Ops:
  0.6 0.9 %copy-start.5 = (f32[1,64]{1,0:T(1,128)S(1)}, f32[1,64]{1,0:T(1,128)}, u32[]{:S(2)}) copy-start(f32[1,64]{1,0:T(1,128)} %sk_ref.1) | copy-start | bytes 772
  0.6 0.9 %copy-start.4 = (s32[1,128]{1,0:T(1,128)S(1)}, s32[1,128]{1,0:T(1,128)}, u32[]{:S(2)}) copy-start(s32[1,128]{1,0:T(1,128)} %st_ref.1) | copy-start | bytes 1540
  1.5 1.2 %copy-start = (bf16[1,128,4096]{2,1,0:T(8,128)(2,1)S(1)}, bf16[1,128,4096]{2,1,0:T(8,128)(2,1)}, u32[]{:S(2)}) copy-start(bf16[1,128,4096]{2,1,0:T(8,128)(2,1)} %e_ref.1) | copy-start | bytes 3145732
  2.7 1.2 %copy-start.1 = (bf16[1,128,4096]{2,1,0:T(8,128)(2,1)S(1)}, bf16[1,128,4096]{2,1,0:T(8,128)(2,1)}, u32[]{:S(2)}) copy-start(bf16[1,128,4096]{2,1,0:T(8,128)(2,1)} %g_ref.1) | copy-start | bytes 3145732
  4.0 0.8 %copy-start.2 = (bf16[1,128,256]{2,1,0:T(8,128)(2,1)S(1)}, bf16[1,128,256]{2,1,0:T(8,128)(2,1)}, u32[]{:S(2)}) copy-start(bf16[1,128,256]{2,1,0:T(8,128)(2,1)} %b_ref.1) | copy-start | bytes 196612
  4.8 0.8 %copy-start.3 = (bf16[1,128,256]{2,1,0:T(8,128)(2,1)S(1)}, bf16[1,128,256]{2,1,0:T(8,128)(2,1)}, u32[]{:S(2)}) copy-start(bf16[1,128,256]{2,1,0:T(8,128)(2,1)} %c_ref.1) | copy-start | bytes 196612

commit v2 on v1

--- a/solution.py
+++ b/solution.py
@@ -9,9 +9,11 @@
 
 BLEND_CHANNELS = 128
 P_SIZE = 64
+CODE_MAX = 32000.0
 N = 128
 GROUPS = 4
 COLS = 512
+LAG = 2
 MESH = pl.DeviceIdType.MESH
 F32 = jnp.float32
 BF16 = jnp.bfloat16
@@ -31,9 +33,11 @@
     e_ref, g_ref, b_ref, c_ref, d_ref, st_ref, sk_ref,
     mixed_ref, grad_ref,
     x_buf, up_out, up_in, down_out, down_in,
+    up_scale_out, up_scale_in, down_scale_out, down_scale_in, got_up, got_down,
     small, centre, lhs_up, lhs_down, low_up, low_down, enter_up, enter_down,
     part_up, part_down, own_up, own_down, gone_row,
     x_send, x_recv, up_send, up_recv, down_send, down_recv,
+    up_scale_send, up_scale_recv, down_scale_send, down_scale_recv,
 ):
     length = e_ref.shape[1]
     chunks = e_ref.shape[2] // cols
@@ -72,19 +76,27 @@
             device_id={"pipe": pipe + 1}, device_id_type=MESH,
         )
 
-    def up_copy(j):
-        return pltpu.make_async_remote_copy(
-            src_ref=up_out.at[j], dst_ref=up_in.at[j],
-            send_sem=up_send.at[j], recv_sem=up_recv.at[j],
-            device_id={"seq": seq + 1}, device_id_type=MESH,
-        )
-
-    def down_copy(j):
-        return pltpu.make_async_remote_copy(
-            src_ref=down_out.at[j], dst_ref=down_in.at[j],
-            send_sem=down_send.at[j], recv_sem=down_recv.at[j],
-            device_id={"seq": seq - 1}, device_id_type=MESH,
-        )
+    def pair(pieces, where):
+        return [
+            pltpu.make_async_remote_copy(
+                src_ref=source, dst_ref=target, send_sem=sent, recv_sem=arrived,
+                device_id=where, device_id_type=MESH,
+            )
+            for source, target, sent, arrived in pieces
+        ]
+
+    def up_copies(j):
+        return pair([
+            (up_scale_out.at[j], up_scale_in.at[j], up_scale_send.at[j], up_scale_recv.at[j]),
+            (up_out.at[j], up_in.at[j], up_send.at[j], up_recv.at[j]),
+        ], {"seq": seq + 1})
+
+    def down_copies(j):
+        return pair([
+            (down_scale_out.at[j], down_scale_in.at[j], down_scale_send.at[j],
+             down_scale_recv.at[j]),
+            (down_out.at[j], down_in.at[j], down_send.at[j], down_recv.at[j]),
+        ], {"seq": seq - 1})
 
     @pl.when(has_next_pipe)
     def _():
@@ -157,96 +169,96 @@
         half = decay[0:1] - shift[0:1]
         return shift, half, gain_wide
 
-    steps = chunks + seq_count - 1
+    steps = chunks + LAG * (seq_count - 1)
 
     @pl.loop(0, steps)
     def _(step):
-        ju = step - seq
-        jd = step - (seq_count - 1 - seq)
+        ju = step - LAG * seq
+        jd = step - LAG * (seq_count - 1 - seq)
         up_on = jnp.logical_and(ju >= 0, ju < chunks)
         down_on = jnp.logical_and(jd >= 0, jd < chunks)
 
-        @pl.when(down_on)
-        def _():
-            q = jd // chunks_per_group
-            shift, half, gain_wide = factors(jd)
-            g = g_ref[0, :, pl.ds(pl.multiple_of(jd * cols, cols), cols)].astype(F32)
-            high, low = split(g * jnp.exp(shift))
+        @pl.when(step < chunks)
+        def _():
+            j = step
+            q = j // chunks_per_group
+            shift, half, gain_wide = factors(j)
+            forth, back = jnp.exp(shift), jnp.exp(-shift)
+            forth_end, forth_in = jnp.exp(shift[length - 1:]), jnp.exp(half)
+            gone = jnp.exp(half + shift[length - 1:]) * gone_row[0:1, 0:1]
+            g = g_ref[0, :, pl.ds(pl.multiple_of(j * cols, cols), cols)].astype(F32)
+            high, low = split(g * forth)
             both = dot(lhs_down[q], jnp.concatenate([high, low], axis=0))
-            back = jnp.exp(-shift)
-            part_down[0] = (both[0:length] + dot(low_down[q], high)) * back + gain_wide * g
-            part_down[1] = back * jnp.exp(shift[length - 1:])
-            own_down[0:N] = both[length:] * jnp.exp(half)
-            own_down[N:N + 8] = jnp.broadcast_to(
-                jnp.exp(half + shift[length - 1:]) * gone_row[0:1, 0:1], (8, cols)
-            )
-
-            @pl.when(seq == seq_count - 1)
-            def _():
-                down_in[jd] = jnp.zeros(down_in.shape[1:], BF16)
-
-        @pl.when(up_on)
-        def _():
-            q = ju // chunks_per_group
+            part_down[j, 0] = (both[0:length] + dot(low_down[q], high)) * back + gain_wide * g
+            part_down[j, 1] = back * forth_end
+            own_down[j, 0:N] = both[length:] * forth_in
+            own_down[j, N:N + 8] = jnp.broadcast_to(gone, (8, cols))
 
             @pl.when(pipe == 0)
             def _():
-                x_buf[ju] = e_ref[0, :, pl.ds(pl.multiple_of(ju * cols, cols), cols)]
+                x_buf[j] = e_ref[0, :, pl.ds(pl.multiple_of(j * cols, cols), cols)]
 
             @pl.when(has_prev_pipe)
             def _():
-                x_copy(ju).wait_recv()
-
-            shift, half, gain_wide = factors(ju)
-            x = x_buf[ju].astype(F32)
-            high, low = split(x * jnp.exp(-shift))
+                x_copy(j).wait_recv()
+
+            x = x_buf[j].astype(F32)
+            high, low = split(x * back)
             both = dot(lhs_up[q], jnp.concatenate([high, low], axis=0))
-            forth = jnp.exp(shift)
-            part_up[0] = (both[0:length] + dot(low_up[q], high)) * forth + gain_wide * x
-            part_up[1] = forth * jnp.exp(half)
-            own_up[0:N] = both[length:] * jnp.exp(shift[length - 1:])
-            own_up[N:N + 8] = jnp.broadcast_to(
-                jnp.exp(half + shift[length - 1:]) * gone_row[0:1, 0:1], (8, cols)
-            )
-
-            @pl.when(seq == 0)
+            part_up[j, 0] = (both[0:length] + dot(low_up[q], high)) * forth + gain_wide * x
+            part_up[j, 1] = forth * forth_in
+            own_up[j, 0:N] = both[length:] * forth_end
+            own_up[j, N:N + 8] = jnp.broadcast_to(gone, (8, cols))
+
+        def relay(on, j, source, target, copies, code_in, scale_in, code_out, scale_out, got, own):
+            @pl.when(on)
             def _():
-                up_in[ju] = jnp.zeros(up_in.shape[1:], BF16)
-
-        @pl.when(jnp.logical_and(down_on, has_next))
-        def _():
-            down_copy(jd).wait_recv()
-
-        @pl.when(jnp.logical_and(down_on, has_prev))
-        def _():
-            got = down_in[jd, 0:N].astype(F32) + down_in[jd, N:].astype(F32)
-            high, low = split(got * own_down[N:N + 1] + own_down[0:N])
-            down_out[jd, 0:N] = high
-            down_out[jd, N:] = low
-            down_copy(jd).start()
-
-        @pl.when(jnp.logical_and(up_on, has_prev))
-        def _():
-            up_copy(ju).wait_recv()
-
-        @pl.when(jnp.logical_and(up_on, has_next))
-        def _():
-            got = up_in[ju, 0:N].astype(F32) + up_in[ju, N:].astype(F32)
-            high, low = split(got * own_up[N:N + 1] + own_up[0:N])
-            up_out[ju, 0:N] = high
-            up_out[ju, N:] = low
-            up_copy(ju).start()
+                @pl.when(jnp.logical_not(source))
+                def _():
+                    got[...] = jnp.zeros(got.shape, F32)
+
+                @pl.when(source)
+                def _():
+                    for copy in copies(j):
+                        copy.wait_recv()
+                    scale = jnp.sum(
+                        jnp.where(row == col, scale_in[j, 0:1], 0.0), axis=1, keepdims=True
+                    )
+                    got[...] = code_in[j].astype(jnp.int32).astype(F32) * scale
+
+                @pl.when(target)
+                def _():
+                    state = got[...] * own[j, N:N + 1] + own[j, 0:N]
+                    largest = jnp.maximum(
+                        jnp.max(jnp.abs(state), axis=1, keepdims=True), 1e-30
+                    )
+                    code = jnp.round(state * (CODE_MAX / largest))
+                    code_out[j] = code.astype(jnp.int32).astype(jnp.int16)
+                    scale = jnp.sum(
+                        jnp.where(row == col, largest * (1.0 / CODE_MAX), 0.0),
+                        axis=0, keepdims=True,
+                    )
+                    scale_out[j] = jnp.broadcast_to(scale, scale_out.shape[1:])
+                    for copy in copies(j):
+                        copy.start()
+
+        relay(down_on, jd, has_next, has_prev, down_copies, down_in, down_scale_in,
+              down_out, down_scale_out, got_down, own_down)
+        relay(up_on, ju, has_prev, has_next, up_copies, up_in, up_scale_in,
+              up_out, up_scale_out, got_up, own_up)
 
         @pl.when(down_on)
         def _():
             q = jd // chunks_per_group
-            total = part_down[0] + dot(enter_down[q], down_in[jd]) * part_down[1]
+            both = jnp.concatenate(split(got_down[...]), axis=0)
+            total = part_down[jd, 0] + dot(enter_down[q], both) * part_down[jd, 1]
             grad_ref[0, :, pl.ds(pl.multiple_of(jd * cols, cols), cols)] = total.astype(BF16)
 
         @pl.when(up_on)
         def _():
             q = ju // chunks_per_group
-            total = part_up[0] + dot(enter_up[q], up_in[ju]) * part_up[1]
+            both = jnp.concatenate(split(got_up[...]), axis=0)
+            total = part_up[ju, 0] + dot(enter_up[q], both) * part_up[ju, 1]
             mixed_ref[0, :, pl.ds(pl.multiple_of(ju * cols, cols), cols)] = total.astype(BF16)
 
     @pl.loop(0, chunks)
@@ -257,11 +269,13 @@
 
         @pl.when(has_next)
         def _():
-            up_copy(j).wait_send()
+            for copy in up_copies(j):
+                copy.wait_send()
 
         @pl.when(has_prev)
         def _():
-            down_copy(j).wait_send()
+            for copy in down_copies(j):
+                copy.wait_send()
 
 
 def body(pipe_count, seq_count, emitted, cotangent, b_proj, c_proj, log_decay, starts, skip):
@@ -282,10 +296,16 @@
         out_specs=(whole, whole),
         scratch_shapes=[
             pltpu.VMEM((chunks, length, cols), BF16),
-            pltpu.VMEM((chunks, 2 * N, cols), BF16),
-            pltpu.VMEM((chunks, 2 * N, cols), BF16),
-            pltpu.VMEM((chunks, 2 * N, cols), BF16),
-            pltpu.VMEM((chunks, 2 * N, cols), BF16),
+            pltpu.VMEM((chunks, N, cols), jnp.int16),
+            pltpu.VMEM((chunks, N, cols), jnp.int16),
+            pltpu.VMEM((chunks, N, cols), jnp.int16),
+            pltpu.VMEM((chunks, N, cols), jnp.int16),
+            pltpu.VMEM((chunks, 8, N), F32),
+            pltpu.VMEM((chunks, 8, N), F32),
+            pltpu.VMEM((chunks, 8, N), F32),
+            pltpu.VMEM((chunks, 8, N), F32),
+            pltpu.VMEM((N, cols), F32),
+            pltpu.VMEM((N, cols), F32),
             pltpu.VMEM((length + 16, heads), BF16),
             pltpu.VMEM((length, length), BF16),
             pltpu.VMEM((group_count, length + N, 2 * length), BF16),
@@ -294,13 +314,14 @@
             pltpu.VMEM((group_count, length, length), BF16),
             pltpu.VMEM((group_count, length, 2 * N), BF16),
             pltpu.VMEM((group_count, length, 2 * N), BF16),
-            pltpu.VMEM((2, length, cols), F32),
-            pltpu.VMEM((2, length, cols), F32),
-            pltpu.VMEM((N + 8, cols), F32),
-            pltpu.VMEM((N + 8, cols), F32),
+            pltpu.VMEM((chunks, 2, length, cols), F32),
+            pltpu.VMEM((chunks, 2, length, cols), F32),
+            pltpu.VMEM((chunks, N + 8, cols), F32),
+            pltpu.VMEM((chunks, N + 8, cols), F32),
             pltpu.VMEM((8, 128), F32),
             dma((chunks,)), dma((chunks,)), dma((chunks,)),
             dma((chunks,)), dma((chunks,)), dma((chunks,)),
+            dma((chunks,)), dma((chunks,)), dma((chunks,)), dma((chunks,)),
         ],
         compiler_params=pltpu.CompilerParams(
             collective_id=0, has_side_effects=True, vmem_limit_bytes=40 * 1024 * 1024

time: 76.6 us -> 50.1 us (0.65)
  Pallas kernels: 68.3 us -> 42.2 us
    pallas_call x1, Pallas kernels: 68.3 us -> 42.2 us  [body(): pl.pallas_call(functools.partial(kernel, pipe_count, seq_count, cols), ou...]
where the time goes in v2:
time: 50.1 us; the launch traced here: 49.8 us
  Pallas kernels  42.2 us (84%)
  local copies, waits for them, and re-layouts  6.91 us (14%)
  between operations  0.68 us (1%)
    pallas_call x1, Pallas kernels, body(): pl.pallas_call(functools.partial(kernel, pipe_count, seq_count, cols), ou...  42.2 us
    unnamed x15, local copies, waits for them, and re-layouts  6.91 us

profile of v2, /device:TPU:0, one launch (start us, length us, event | category | flops | bytes accessed | tf_op | source)
XLA Modules:
  0.0 49.8 jit_solution(17874623298743671714)
XLA Ops:
  0.6 0.0 copy-start.5
  0.6 0.0 copy-start.4
  0.7 0.8 %copy.9.d_ref = bf16[1,128,64]{2,1,0:T(8,128)(2,1)S(1)} copy(bf16[1,128,64]{1,2,0:T(8,128)(2,1)} %param.11) | data formatting | bytes 32768 | tf_op args[4]
  1.5 0.0 copy-done.5
  1.5 0.0 copy-done.4
  1.5 0.0 copy-start
  1.5 1.2 %copy-done = bf16[1,128,4096]{2,1,0:T(8,128)(2,1)S(1)} copy-done((bf16[1,128,4096]{2,1,0:T(8,128)(2,1)S(1)}, bf16[1,128,4096]{2,1,0:T(8,128)(2,1)}, u32[]{:S(2)}) %copy-start) | copy-done | bytes 1048600
  2.7 0.0 copy-start.1
  2.7 1.2 %copy-done.1 = bf16[1,128,4096]{2,1,0:T(8,128)(2,1)S(1)} copy-done((bf16[1,128,4096]{2,1,0:T(8,128)(2,1)S(1)}, bf16[1,128,4096]{2,1,0:T(8,128)(2,1)}, u32[]{:S(2)}) %copy-start.1) | copy-done | bytes 1048600
  4.0 0.0 copy-start.2
  4.0 0.8 %copy-done.2 = bf16[1,128,256]{2,1,0:T(8,128)(2,1)S(1)} copy-done((bf16[1,128,256]{2,1,0:T(8,128)(2,1)S(1)}, bf16[1,128,256]{2,1,0:T(8,128)(2,1)}, u32[]{:S(2)}) %copy-start.2) | copy-done | bytes 65560
  4.8 0.0 copy-start.3
  4.8 0.8 %copy-done.3 = bf16[1,128,256]{2,1,0:T(8,128)(2,1)S(1)} copy-done((bf16[1,128,256]{2,1,0:T(8,128)(2,1)S(1)}, bf16[1,128,256]{2,1,0:T(8,128)(2,1)}, u32[]{:S(2)}) %copy-start.3) | copy-done | bytes 65560
  5.6 42.2 %shard_map.86 = (bf16[1,128,4096]{2,1,0:T(8,128)(2,1)S(1)}, bf16[1,128,4096]{2,1,0:T(8,128)(2,1)S(1)}) custom-call(bf16[1,128,4096]{2,1,0:T(8,128)(2,1)S(1)} %copy-done, bf16[1,128,4096]{2,1,0:T(8,128)(2,1)S(1)} %copy-done.1, bf16[1,128,256]{2,1,0:T(8,128)(2,1)S(1)} %copy-done.2, bf16[1,128,256]{2,1,0:T(8,128)(2,1)S(1)} %copy-done.3, ...), custom_call_target="tpu_custom_call" | custom-call | tf_op jit(solution)/shard_map/pallas_call | solution.py:289
  47.9 1.0 %copy.12 = bf16[1,128,4096]{2,1,0:T(8,128)(2,1)} copy(bf16[1,128,4096]{2,1,0:T(8,128)(2,1)S(1)} %get-tuple-element.4) | data formatting | bytes 2097152
  48.8 1.0 %copy.13 = bf16[1,128,4096]{2,1,0:T(8,128)(2,1)} copy(bf16[1,128,4096]{2,1,0:T(8,128)(2,1)S(1)} %get-tuple-element.5) | data formatting | bytes 2097152
Async XLA Ops:
  0.6 0.9 %copy-start.5 = (f32[1,64]{1,0:T(1,128)S(1)}, f32[1,64]{1,0:T(1,128)}, u32[]{:S(2)}) copy-start(f32[1,64]{1,0:T(1,128)} %sk_ref.1) | copy-start | bytes 772
  0.6 0.9 %copy-start.4 = (s32[1,128]{1,0:T(1,128)S(1)}, s32[1,128]{1,0:T(1,128)}, u32[]{:S(2)}) copy-start(s32[1,128]{1,0:T(1,128)} %st_ref.1) | copy-start | bytes 1540
  1.5 1.2 %copy-start = (bf16[1,128,4096]{2,1,0:T(8,128)(2,1)S(1)}, bf16[1,128,4096]{2,1,0:T(8,128)(2,1)}, u32[]{:S(2)}) copy-start(bf16[1,128,4096]{2,1,0:T(8,128)(2,1)} %e_ref.1) | copy-start | bytes 3145732
  2.7 1.2 %copy-start.1 = (bf16[1,128,4096]{2,1,0:T(8,128)(2,1)S(1)}, bf16[1,128,4096]{2,1,0:T(8,128)(2,1)}, u32[]{:S(2)}) copy-start(bf16[1,128,4096]{2,1,0:T(8,128)(2,1)} %g_ref.1) | copy-start | bytes 3145732
  4.0 0.8 %copy-start.2 = (bf16[1,128,256]{2,1,0:T(8,128)(2,1)S(1)}, bf16[1,128,256]{2,1,0:T(8,128)(2,1)}, u32[]{:S(2)}) copy-start(bf16[1,128,256]{2,1,0:T(8,128)(2,1)} %b_ref.1) | copy-start | bytes 196612
  4.8 0.8 %copy-start.3 = (bf16[1,128,256]{2,1,0:T(8,128)(2,1)S(1)}, bf16[1,128,256]{2,1,0:T(8,128)(2,1)}, u32[]{:S(2)}) copy-start(bf16[1,128,256]{2,1,0:T(8,128)(2,1)} %c_ref.1) | copy-start | bytes 196612

commit v3 on v2

--- a/solution.py
+++ b/solution.py
@@ -14,6 +14,7 @@
 GROUPS = 4
 COLS = 512
 LAG = 2
+UP_DELAY = 0
 MESH = pl.DeviceIdType.MESH
 F32 = jnp.float32
 BF16 = jnp.bfloat16
@@ -169,46 +170,14 @@
         half = decay[0:1] - shift[0:1]
         return shift, half, gain_wide
 
-    steps = chunks + LAG * (seq_count - 1)
+    steps = chunks + LAG * (seq_count - 1) + UP_DELAY
 
     @pl.loop(0, steps)
     def _(step):
-        ju = step - LAG * seq
+        ju = step - UP_DELAY - LAG * seq
         jd = step - LAG * (seq_count - 1 - seq)
         up_on = jnp.logical_and(ju >= 0, ju < chunks)
         down_on = jnp.logical_and(jd >= 0, jd < chunks)
-
-        @pl.when(step < chunks)
-        def _():
-            j = step
-            q = j // chunks_per_group
-            shift, half, gain_wide = factors(j)
-            forth, back = jnp.exp(shift), jnp.exp(-shift)
-            forth_end, forth_in = jnp.exp(shift[length - 1:]), jnp.exp(half)
-            gone = jnp.exp(half + shift[length - 1:]) * gone_row[0:1, 0:1]
-            g = g_ref[0, :, pl.ds(pl.multiple_of(j * cols, cols), cols)].astype(F32)
-            high, low = split(g * forth)
-            both = dot(lhs_down[q], jnp.concatenate([high, low], axis=0))
-            part_down[j, 0] = (both[0:length] + dot(low_down[q], high)) * back + gain_wide * g
-            part_down[j, 1] = back * forth_end
-            own_down[j, 0:N] = both[length:] * forth_in
-            own_down[j, N:N + 8] = jnp.broadcast_to(gone, (8, cols))
-
-            @pl.when(pipe == 0)
-            def _():
-                x_buf[j] = e_ref[0, :, pl.ds(pl.multiple_of(j * cols, cols), cols)]
-
-            @pl.when(has_prev_pipe)
-            def _():
-                x_copy(j).wait_recv()
-
-            x = x_buf[j].astype(F32)
-            high, low = split(x * back)
-            both = dot(lhs_up[q], jnp.concatenate([high, low], axis=0))
-            part_up[j, 0] = (both[0:length] + dot(low_up[q], high)) * forth + gain_wide * x
-            part_up[j, 1] = forth * forth_in
-            own_up[j, 0:N] = both[length:] * forth_end
-            own_up[j, N:N + 8] = jnp.broadcast_to(gone, (8, cols))
 
         def relay(on, j, source, target, copies, code_in, scale_in, code_out, scale_out, got, own):
             @pl.when(on)
@@ -242,8 +211,52 @@
                     for copy in copies(j):
                         copy.start()
 
+        @pl.when(step < chunks)
+        def _():
+            j = step
+            q = j // chunks_per_group
+            shift, half, gain_wide = factors(j)
+            forth, back = jnp.exp(shift), jnp.exp(-shift)
+            forth_end, forth_in = jnp.exp(shift[length - 1:]), jnp.exp(half)
+            gone = jnp.exp(half + shift[length - 1:]) * gone_row[0:1, 0:1]
+            g = g_ref[0, :, pl.ds(pl.multiple_of(j * cols, cols), cols)].astype(F32)
+            high, low = split(g * forth)
+            both = dot(lhs_down[q], jnp.concatenate([high, low], axis=0))
+            part_down[j, 0] = (both[0:length] + dot(low_down[q], high)) * back + gain_wide * g
+            part_down[j, 1] = back * forth_end
+            own_down[j, 0:N] = both[length:] * forth_in
+            own_down[j, N:N + 8] = jnp.broadcast_to(gone, (8, cols))
+
         relay(down_on, jd, has_next, has_prev, down_copies, down_in, down_scale_in,
               down_out, down_scale_out, got_down, own_down)
+
+        j_up = step - UP_DELAY
+
+        @pl.when(jnp.logical_and(j_up >= 0, j_up < chunks))
+        def _():
+            j = j_up
+            q = j // chunks_per_group
+            shift, half, gain_wide = factors(j)
+            forth, back = jnp.exp(shift), jnp.exp(-shift)
+            forth_end, forth_in = jnp.exp(shift[length - 1:]), jnp.exp(half)
+            gone = jnp.exp(half + shift[length - 1:]) * gone_row[0:1, 0:1]
+
+            @pl.when(pipe == 0)
+            def _():
+                x_buf[j] = e_ref[0, :, pl.ds(pl.multiple_of(j * cols, cols), cols)]
+
+            @pl.when(has_prev_pipe)
+            def _():
+                x_copy(j).wait_recv()
+
+            x = x_buf[j].astype(F32)
+            high, low = split(x * back)
+            both = dot(lhs_up[q], jnp.concatenate([high, low], axis=0))
+            part_up[j, 0] = (both[0:length] + dot(low_up[q], high)) * forth + gain_wide * x
+            part_up[j, 1] = forth * forth_in
+            own_up[j, 0:N] = both[length:] * forth_end
+            own_up[j, N:N + 8] = jnp.broadcast_to(gone, (8, cols))
+
         relay(up_on, ju, has_prev, has_next, up_copies, up_in, up_scale_in,
               up_out, up_scale_out, got_up, own_up)
 

time: 50.1 us -> 49.8 us (level)
  no operation moved by 1% of the time
where the time goes in v3:
time: 49.8 us; the launch traced here: 49.5 us
  Pallas kernels  41.9 us (84%)
  local copies, waits for them, and re-layouts  6.91 us (14%)
  between operations  0.68 us (1%)
    pallas_call x1, Pallas kernels, body(): pl.pallas_call(functools.partial(kernel, pipe_count, seq_count, cols), ou...  41.9 us
    unnamed x15, local copies, waits for them, and re-layouts  6.91 us

profile of v3, /device:TPU:0, one launch (start us, length us, event | category | flops | bytes accessed | tf_op | source)
XLA Modules:
  0.0 49.5 jit_solution(10392255090778388132)
XLA Ops:
  0.6 0.0 copy-start.5
  0.6 0.0 copy-start.4
  0.7 0.8 %copy.9.d_ref = bf16[1,128,64]{2,1,0:T(8,128)(2,1)S(1)} copy(bf16[1,128,64]{1,2,0:T(8,128)(2,1)} %param.11) | data formatting | bytes 32768 | tf_op args[4]
  1.5 0.0 copy-done.5
  1.5 0.0 copy-done.4
  1.5 0.0 copy-start
  1.5 1.2 %copy-done = bf16[1,128,4096]{2,1,0:T(8,128)(2,1)S(1)} copy-done((bf16[1,128,4096]{2,1,0:T(8,128)(2,1)S(1)}, bf16[1,128,4096]{2,1,0:T(8,128)(2,1)}, u32[]{:S(2)}) %copy-start) | copy-done | bytes 1048600
  2.7 0.0 copy-start.1
  2.7 1.2 %copy-done.1 = bf16[1,128,4096]{2,1,0:T(8,128)(2,1)S(1)} copy-done((bf16[1,128,4096]{2,1,0:T(8,128)(2,1)S(1)}, bf16[1,128,4096]{2,1,0:T(8,128)(2,1)}, u32[]{:S(2)}) %copy-start.1) | copy-done | bytes 1048600
  4.0 0.0 copy-start.2
  4.0 0.8 %copy-done.2 = bf16[1,128,256]{2,1,0:T(8,128)(2,1)S(1)} copy-done((bf16[1,128,256]{2,1,0:T(8,128)(2,1)S(1)}, bf16[1,128,256]{2,1,0:T(8,128)(2,1)}, u32[]{:S(2)}) %copy-start.2) | copy-done | bytes 65560
  4.8 0.0 copy-start.3
  4.8 0.8 %copy-done.3 = bf16[1,128,256]{2,1,0:T(8,128)(2,1)S(1)} copy-done((bf16[1,128,256]{2,1,0:T(8,128)(2,1)S(1)}, bf16[1,128,256]{2,1,0:T(8,128)(2,1)}, u32[]{:S(2)}) %copy-start.3) | copy-done | bytes 65560
  5.6 41.9 %shard_map.86 = (bf16[1,128,4096]{2,1,0:T(8,128)(2,1)S(1)}, bf16[1,128,4096]{2,1,0:T(8,128)(2,1)S(1)}) custom-call(bf16[1,128,4096]{2,1,0:T(8,128)(2,1)S(1)} %copy-done, bf16[1,128,4096]{2,1,0:T(8,128)(2,1)S(1)} %copy-done.1, bf16[1,128,256]{2,1,0:T(8,128)(2,1)S(1)} %copy-done.2, bf16[1,128,256]{2,1,0:T(8,128)(2,1)S(1)} %copy-done.3, ...), custom_call_target="tpu_custom_call" | custom-call | tf_op jit(solution)/shard_map/pallas_call | solution.py:302
  47.5 1.0 %copy.12 = bf16[1,128,4096]{2,1,0:T(8,128)(2,1)} copy(bf16[1,128,4096]{2,1,0:T(8,128)(2,1)S(1)} %get-tuple-element.4) | data formatting | bytes 2097152
  48.5 1.0 %copy.13 = bf16[1,128,4096]{2,1,0:T(8,128)(2,1)} copy(bf16[1,128,4096]{2,1,0:T(8,128)(2,1)S(1)} %get-tuple-element.5) | data formatting | bytes 2097152
Async XLA Ops:
  0.6 0.9 %copy-start.5 = (f32[1,64]{1,0:T(1,128)S(1)}, f32[1,64]{1,0:T(1,128)}, u32[]{:S(2)}) copy-start(f32[1,64]{1,0:T(1,128)} %sk_ref.1) | copy-start | bytes 772
  0.6 0.9 %copy-start.4 = (s32[1,128]{1,0:T(1,128)S(1)}, s32[1,128]{1,0:T(1,128)}, u32[]{:S(2)}) copy-start(s32[1,128]{1,0:T(1,128)} %st_ref.1) | copy-start | bytes 1540
  1.5 1.2 %copy-start = (bf16[1,128,4096]{2,1,0:T(8,128)(2,1)S(1)}, bf16[1,128,4096]{2,1,0:T(8,128)(2,1)}, u32[]{:S(2)}) copy-start(bf16[1,128,4096]{2,1,0:T(8,128)(2,1)} %e_ref.1) | copy-start | bytes 3145732
  2.7 1.2 %copy-start.1 = (bf16[1,128,4096]{2,1,0:T(8,128)(2,1)S(1)}, bf16[1,128,4096]{2,1,0:T(8,128)(2,1)}, u32[]{:S(2)}) copy-start(bf16[1,128,4096]{2,1,0:T(8,128)(2,1)} %g_ref.1) | copy-start | bytes 3145732
  4.0 0.8 %copy-start.2 = (bf16[1,128,256]{2,1,0:T(8,128)(2,1)S(1)}, bf16[1,128,256]{2,1,0:T(8,128)(2,1)}, u32[]{:S(2)}) copy-start(bf16[1,128,256]{2,1,0:T(8,128)(2,1)} %b_ref.1) | copy-start | bytes 196612
  4.8 0.8 %copy-start.3 = (bf16[1,128,256]{2,1,0:T(8,128)(2,1)S(1)}, bf16[1,128,256]{2,1,0:T(8,128)(2,1)}, u32[]{:S(2)}) copy-start(bf16[1,128,256]{2,1,0:T(8,128)(2,1)} %c_ref.1) | copy-start | bytes 196612

commit v4 on v3

--- a/solution.py
+++ b/solution.py
@@ -203,13 +203,14 @@
                     )
                     code = jnp.round(state * (CODE_MAX / largest))
                     code_out[j] = code.astype(jnp.int32).astype(jnp.int16)
+                    scale_copy, code_copy = copies(j)
+                    code_copy.start()
                     scale = jnp.sum(
                         jnp.where(row == col, largest * (1.0 / CODE_MAX), 0.0),
                         axis=0, keepdims=True,
                     )
                     scale_out[j] = jnp.broadcast_to(scale, scale_out.shape[1:])
-                    for copy in copies(j):
-                        copy.start()
+                    scale_copy.start()
 
         @pl.when(step < chunks)
         def _():

time: 49.8 us -> 49.8 us (level)
  no operation moved by 1% of the time
where the time goes in v4:
time: 49.8 us; the launch traced here: 49.5 us
  Pallas kernels  41.9 us (84%)
  local copies, waits for them, and re-layouts  6.91 us (14%)
  between operations  0.68 us (1%)
    pallas_call x1, Pallas kernels, body(): pl.pallas_call(functools.partial(kernel, pipe_count, seq_count, cols), ou...  41.9 us
    unnamed x15, local copies, waits for them, and re-layouts  6.91 us

profile of v4, /device:TPU:0, one launch (start us, length us, event | category | flops | bytes accessed | tf_op | source)
XLA Modules:
  0.0 49.5 jit_solution(1250686824668913043)
XLA Ops:
  0.6 0.0 copy-start.5
  0.6 0.0 copy-start.4
  0.7 0.8 %copy.9.d_ref = bf16[1,128,64]{2,1,0:T(8,128)(2,1)S(1)} copy(bf16[1,128,64]{1,2,0:T(8,128)(2,1)} %param.11) | data formatting | bytes 32768 | tf_op args[4]
  1.5 0.0 copy-done.5
  1.5 0.0 copy-done.4
  1.5 0.0 copy-start
  1.5 1.2 %copy-done = bf16[1,128,4096]{2,1,0:T(8,128)(2,1)S(1)} copy-done((bf16[1,128,4096]{2,1,0:T(8,128)(2,1)S(1)}, bf16[1,128,4096]{2,1,0:T(8,128)(2,1)}, u32[]{:S(2)}) %copy-start) | copy-done | bytes 1048600
  2.7 0.0 copy-start.1
  2.7 1.2 %copy-done.1 = bf16[1,128,4096]{2,1,0:T(8,128)(2,1)S(1)} copy-done((bf16[1,128,4096]{2,1,0:T(8,128)(2,1)S(1)}, bf16[1,128,4096]{2,1,0:T(8,128)(2,1)}, u32[]{:S(2)}) %copy-start.1) | copy-done | bytes 1048600
  4.0 0.0 copy-start.2
  4.0 0.8 %copy-done.2 = bf16[1,128,256]{2,1,0:T(8,128)(2,1)S(1)} copy-done((bf16[1,128,256]{2,1,0:T(8,128)(2,1)S(1)}, bf16[1,128,256]{2,1,0:T(8,128)(2,1)}, u32[]{:S(2)}) %copy-start.2) | copy-done | bytes 65560
  4.8 0.0 copy-start.3
  4.8 0.8 %copy-done.3 = bf16[1,128,256]{2,1,0:T(8,128)(2,1)S(1)} copy-done((bf16[1,128,256]{2,1,0:T(8,128)(2,1)S(1)}, bf16[1,128,256]{2,1,0:T(8,128)(2,1)}, u32[]{:S(2)}) %copy-start.3) | copy-done | bytes 65560
  5.6 41.9 %shard_map.86 = (bf16[1,128,4096]{2,1,0:T(8,128)(2,1)S(1)}, bf16[1,128,4096]{2,1,0:T(8,128)(2,1)S(1)}) custom-call(bf16[1,128,4096]{2,1,0:T(8,128)(2,1)S(1)} %copy-done, bf16[1,128,4096]{2,1,0:T(8,128)(2,1)S(1)} %copy-done.1, bf16[1,128,256]{2,1,0:T(8,128)(2,1)S(1)} %copy-done.2, bf16[1,128,256]{2,1,0:T(8,128)(2,1)S(1)} %copy-done.3, ...), custom_call_target="tpu_custom_call" | custom-call | tf_op jit(solution)/shard_map/pallas_call | solution.py:303
  47.5 1.0 %copy.12 = bf16[1,128,4096]{2,1,0:T(8,128)(2,1)} copy(bf16[1,128,4096]{2,1,0:T(8,128)(2,1)S(1)} %get-tuple-element.4) | data formatting | bytes 2097152
  48.5 1.0 %copy.13 = bf16[1,128,4096]{2,1,0:T(8,128)(2,1)} copy(bf16[1,128,4096]{2,1,0:T(8,128)(2,1)S(1)} %get-tuple-element.5) | data formatting | bytes 2097152
Async XLA Ops:
  0.6 0.9 %copy-start.5 = (f32[1,64]{1,0:T(1,128)S(1)}, f32[1,64]{1,0:T(1,128)}, u32[]{:S(2)}) copy-start(f32[1,64]{1,0:T(1,128)} %sk_ref.1) | copy-start | bytes 772
  0.6 0.9 %copy-start.4 = (s32[1,128]{1,0:T(1,128)S(1)}, s32[1,128]{1,0:T(1,128)}, u32[]{:S(2)}) copy-start(s32[1,128]{1,0:T(1,128)} %st_ref.1) | copy-start | bytes 1540
  1.5 1.2 %copy-start = (bf16[1,128,4096]{2,1,0:T(8,128)(2,1)S(1)}, bf16[1,128,4096]{2,1,0:T(8,128)(2,1)}, u32[]{:S(2)}) copy-start(bf16[1,128,4096]{2,1,0:T(8,128)(2,1)} %e_ref.1) | copy-start | bytes 3145732
  2.7 1.2 %copy-start.1 = (bf16[1,128,4096]{2,1,0:T(8,128)(2,1)S(1)}, bf16[1,128,4096]{2,1,0:T(8,128)(2,1)}, u32[]{:S(2)}) copy-start(bf16[1,128,4096]{2,1,0:T(8,128)(2,1)} %g_ref.1) | copy-start | bytes 3145732
  4.0 0.8 %copy-start.2 = (bf16[1,128,256]{2,1,0:T(8,128)(2,1)S(1)}, bf16[1,128,256]{2,1,0:T(8,128)(2,1)}, u32[]{:S(2)}) copy-start(bf16[1,128,256]{2,1,0:T(8,128)(2,1)} %b_ref.1) | copy-start | bytes 196612
  4.8 0.8 %copy-start.3 = (bf16[1,128,256]{2,1,0:T(8,128)(2,1)S(1)}, bf16[1,128,256]{2,1,0:T(8,128)(2,1)}, u32[]{:S(2)}) copy-start(bf16[1,128,256]{2,1,0:T(8,128)(2,1)} %c_ref.1) | copy-start | bytes 196612
